TPU v7x, 128 devices: a whole 4x4x4 slice. The times are simulated.
128 devices in a mesh: seq: 64 (over x, y_lo, z, core), dp: 2 (over y_hi).
Axes of the slice: x: 4, y: 4 (y_hi: 2, y_lo: 2; y = y_hi * 2 + y_lo), z: 4, core: 2. Of those that a mesh axis runs over, the one named last changes fastest.
Arguments:
- inputs: float32 [2, 32, 524288], P('dp', None, 'seq'), may hold values from -6 to 6
- grad_out: float32 [2, 32, 524288], P('dp', None, 'seq'), may hold values from -6 to 6
- filters: float32 [32, 524288], P(None, 'seq'), may hold values from -6 to 6
- skip: float32 [32], replicated, may hold values from 0.5 to 1.5
Outputs:
- grad_in: float32 [2, 32, 524288], P('dp', None, 'seq')
- filter_grad: float32 [32, 524288], P(None, 'seq')
All inputs are finite; a program needn't handle non-finite values.
Results may differ from a plain program's by a relative error of at most 0.000098.
Values sent between devices are 32-bit elements; how exact they have to be, the bound alone decides.
A program may use at most 192 MiB of HBM per device.

v0:
```python
import math

import jax
import jax.numpy as jnp
from jax import lax
from jax.sharding import PartitionSpec as P

highest = lax.Precision.HIGHEST


def phase_table(first_len, second_len, modulus, direction):
    first = jnp.arange(first_len, dtype=jnp.int32)[:, None]
    second = jnp.arange(second_len, dtype=jnp.int32)[None, :]
    angles = 2.0 * math.pi / modulus * (first * second % modulus).astype(jnp.float32)
    return (jnp.cos(angles), direction * jnp.sin(angles))


def twist(real_part, imag_part, cosines, sines):
    return (real_part * cosines - imag_part * sines, real_part * sines + imag_part * cosines)


def complex_section(real_part, imag_part, cosines, sines, form):
    real_cos = jnp.einsum(form, real_part, cosines, precision=highest)
    real_sin = jnp.einsum(form, real_part, sines, precision=highest)
    imag_cos = jnp.einsum(form, imag_part, cosines, precision=highest)
    imag_sin = jnp.einsum(form, imag_part, sines, precision=highest)
    return (real_cos - imag_sin, real_sin + imag_cos)


def local_forward(stacked):
    length_b = stacked.shape[-1]
    first_radix = min(128, length_b)
    second_radix = length_b // first_radix
    shaped = stacked.reshape(stacked.shape[:-1] + (first_radix, second_radix))
    real_part, imag_part = (shaped[0], shaped[1])
    cos_first, sin_first = phase_table(first_radix, first_radix, first_radix, -1.0)
    real_part, imag_part = complex_section(
        real_part, imag_part, cos_first, sin_first, "...ab,ac->...cb"
    )
    cos_twist, sin_twist = phase_table(first_radix, second_radix, length_b, -1.0)
    real_part, imag_part = twist(real_part, imag_part, cos_twist, sin_twist)
    cos_second, sin_second = phase_table(second_radix, second_radix, second_radix, -1.0)
    real_part, imag_part = complex_section(
        real_part, imag_part, cos_second, sin_second, "...cb,bd->...cd"
    )
    return jnp.stack([real_part, imag_part])


def local_inverse(stacked, groups):
    first_radix = stacked.shape[-2]
    second_radix = stacked.shape[-1]
    length_b = first_radix * second_radix
    real_part, imag_part = (stacked[0], stacked[1])
    cos_second, sin_second = phase_table(second_radix, second_radix, second_radix, 1.0)
    real_part, imag_part = complex_section(
        real_part, imag_part, cos_second, sin_second, "...cd,db->...cb"
    )
    cos_twist, sin_twist = phase_table(first_radix, second_radix, length_b, 1.0)
    real_part, imag_part = twist(real_part, imag_part, cos_twist, sin_twist)
    cos_first, sin_first = phase_table(first_radix, first_radix, first_radix, 1.0)
    real_part, imag_part = complex_section(
        real_part, imag_part, cos_first, sin_first, "...cb,ca->...ab"
    )
    real_part = real_part.reshape(real_part.shape[:-2] + (length_b,))
    imag_part = imag_part.reshape(imag_part.shape[:-2] + (length_b,))
    per_device = stacked.shape[2]
    modulus = 2 * length_b * groups
    freq_index = lax.axis_index("seq") * per_device + jnp.arange(per_device, dtype=jnp.int32)
    positions = jnp.arange(length_b, dtype=jnp.int32)
    angles = (
        2.0
        * math.pi
        / modulus
        * (freq_index[:, None] * positions[None, :] % modulus).astype(jnp.float32)
    )
    real_part, imag_part = twist(real_part, imag_part, jnp.cos(angles), jnp.sin(angles))
    return jnp.stack([real_part, imag_part])


def conj_product(left, right):
    real_part = left[0] * right[0] + left[1] * right[1]
    imag_part = left[1] * right[0] - left[0] * right[1]
    return jnp.stack([real_part, imag_part])


def outer_forward(block):
    groups = block.shape[1]
    piece = block.shape[2]
    modulus = 2 * groups * groups * piece
    cos_outer, sin_outer = phase_table(groups, 2 * groups, 2 * groups, -1.0)
    positions = lax.axis_index("seq") * piece + jnp.arange(piece, dtype=jnp.int32)
    freq_index = jnp.arange(2 * groups, dtype=jnp.int32)
    angles = (
        2.0
        * math.pi
        / modulus
        * (freq_index[:, None] * positions[None, :] % modulus).astype(jnp.float32)
    )
    cos_twist = jnp.cos(angles)
    sin_twist = -jnp.sin(angles)
    real_part = jnp.einsum("inm,nk->ikm", block, cos_outer, precision=highest)
    imag_part = jnp.einsum("inm,nk->ikm", block, sin_outer, precision=highest)
    real_part, imag_part = twist(real_part, imag_part, cos_twist, sin_twist)
    return jnp.stack([real_part, imag_part])


def outer_inverse(block):
    wide = block.shape[2]
    groups = wide // 2
    piece = block.shape[3]
    seq_length = groups * groups * piece
    factor = 1.0 / (math.sqrt(seq_length) * 2.0 * seq_length)
    cos_outer, sin_outer = phase_table(wide, groups, wide, 1.0)
    real_part = jnp.einsum("ikm,kn->inm", block[0], cos_outer, precision=highest)
    imag_part = jnp.einsum("ikm,kn->inm", block[1], sin_outer, precision=highest)
    return factor * (real_part - imag_part)


def shards(inputs, grad_out, filters, skip):
    channels = filters.shape[0]
    length_b = filters.shape[1]
    groups = lax.axis_size("seq")
    piece = length_b // groups
    in_rows = inputs.reshape(channels, groups, piece)
    grad_rows = grad_out.reshape(channels, groups, piece)
    filter_rows_in = filters.reshape(channels, groups, piece)
    joined = jnp.concatenate([in_rows, grad_rows, filter_rows_in], axis=0)
    mixed = outer_forward(lax.all_to_all(joined, "seq", split_axis=1, concat_axis=1, tiled=True))
    spectra = local_forward(lax.all_to_all(mixed, "seq", split_axis=2, concat_axis=3, tiled=True))
    in_spec = spectra[:, :channels]
    grad_spec = spectra[:, channels : 2 * channels]
    filter_spec = spectra[:, 2 * channels :]
    input_cross = conj_product(grad_spec, filter_spec)
    filter_part = conj_product(grad_spec, in_spec)
    filter_cross = lax.psum(filter_part, "dp")
    turned = local_inverse(jnp.concatenate([input_cross, filter_cross], axis=1), groups)
    back_rows = outer_inverse(
        lax.all_to_all(turned, "seq", split_axis=3, concat_axis=2, tiled=True)
    )
    back_all = lax.all_to_all(back_rows, "seq", split_axis=1, concat_axis=2, tiled=True)
    conv_rows = back_all[:channels]
    filter_back = back_all[channels:]
    grad_in = conv_rows.reshape(1, channels, length_b) + skip[None, :, None] * grad_out
    filter_grad = filter_back.reshape(filter_back.shape[0], length_b)
    return (grad_in, filter_grad)


def solution(mesh):
    return jax.shard_map(
        shards,
        mesh=mesh,
        in_specs=(P("dp", None, "seq"), P("dp", None, "seq"), P(None, "seq"), P()),
        out_specs=(P("dp", None, "seq"), P(None, "seq")),
        check_vma=False,
    )
```

profile of v0, /device:TPU:1, one launch (start us, length us, event | category | flops | bytes accessed | tf_op | source)
XLA Modules:
  0.0 895.6 jit_solution(12002312163057869613)
XLA Ops:
  7.2 1.5 copy.66
  8.7 1.4 copy.67
  10.1 0.2 copy.68
  10.3 0.4 pad_maximum_fusion.4
  10.7 3.5 copy.39
  14.2 11.2 %all-to-all-start = ((f32[96,64,128]{2,0,1:T(8,128)}), f32[96,64,128]{2,0,1:T(8,128)S(1)}, u32[]{:S(2)}, u32[]{:S(2)}) async-start(f32[96,64,128]{2,0,1:T(8,128)} %copy.39), calls=%async_computation | async-start | bytes 6291456 | tf_op jit(solution)/shard_map/all_to_all | solution.py:128
  25.4 0.3 fusion.98
  25.7 39.6 %all-to-all-done = f32[96,64,128]{2,0,1:T(8,128)S(1)} async-done(((f32[96,64,128]{2,0,1:T(8,128)}), f32[96,64,128]{2,0,1:T(8,128)S(1)}, u32[]{:S(2)}, u32[]{:S(2)}) %all-to-all-start) | async-done | bytes 3145760 | tf_op jit(solution)/shard_map/all_to_all | solution.py:128
  65.2 7.0 fusion.12
  72.3 12.4 %subtract_bitcast_fusion.2 = (f32[1,96,128,128]{3,2,1,0:T(8,128)}, f32[1,96,128,128]{3,2,1,0:T(8,128)}) fusion(f32[128,96,128]{2,0,1:T(8,128)S(1)} %fusion.12, f32[128,128]{1,0:T(8,128)S(1)} %get-tuple-element.21, f32[128,128]{1,0:T(8,128)S(1)} %get-tuple-element.20, f32[96,64,128]{2,0,1:T(8,128)S(1)} %all-to-all-done), kind=kOutput, calls=%fused_computation.8 | convolution fusion | flops 1217511424 | bytes 22151168 | tf_op jit(solution)/shard_map/inm,nk->ikm/dot_general | solution.py:101
  84.7 11.3 %pad_maximum_fusion = f32[2,96,128,128]{3,2,1,0:T(8,128)} fusion(f32[1,96,128,128]{3,2,1,0:T(8,128)} %get-tuple-element.7, f32[1,96,128,128]{3,2,1,0:T(8,128)} %get-tuple-element.6), kind=kLoop, calls=%fused_computation | loop fusion | flops 3145728 | bytes 25165824 | tf_op jit(solution)/shard_map/stack | solution.py:104
  96.0 16.4 %copy.42 = f32[2,96,128,128]{3,1,0,2:T(8,128)} copy(f32[2,96,128,128]{3,2,1,0:T(8,128)} %pad_maximum_fusion) | data formatting | bytes 25165824 | tf_op jit(solution)/shard_map/stack | solution.py:104
  112.4 7.0 all-to-all-start.1
  119.4 0.1 broadcast_multiply_fusion
  119.6 160.2 %all-to-all-done.1 = f32[2,96,128,128]{3,1,0,2:T(8,128)} async-done(((f32[2,96,128,128]{3,1,0,2:T(8,128)}), f32[2,96,128,128]{3,1,0,2:T(8,128)}, u32[]{:S(2)}, u32[]{:S(2)}) %all-to-all-start.1) | async-done | bytes 12582944 | tf_op jit(solution)/shard_map/all_to_all | solution.py:129
  279.8 15.0 %copy.43 = f32[2,96,64,2,128]{1,4,2,3,0:T(8,128)} copy(f32[2,96,64,2,128]{4,1,0,3,2:T(8,128)} %bitcast.10) | data formatting | bytes 25165824 | tf_op jit(solution)/shard_map/all_to_all | solution.py:129
  294.8 10.9 %fusion.215 = (f32[1,96,2,64,128]{1,4,3,2,0:T(8,128)}, f32[1,96,2,64,128]{1,4,3,2,0:T(8,128)}) fusion(f32[2,96,2,64,128]{1,4,3,2,0:T(8,128)} %bitcast.137), kind=kLoop, calls=%fused_computation.243 | loop fusion | bytes 25165824 | tf_op jit(solution)/shard_map/slice | solution.py:35
  305.7 8.4 copy.45
  314.1 9.6 %fusion.37 = f32[128,96,2,64]{0,1,3,2:T(8,128)} fusion(f32[96,2,128,64]{2,0,3,1:T(8,128)} %copy.45), kind=kOutput, calls=%fused_computation.69 | convolution fusion | flops 2416164864 | bytes 12582912 | tf_op jit(solution)/shard_map/...ab,ac->...cb/dot_general | solution.py:26
  323.7 7.4 fusion.41
  331.1 8.4 copy.44
  339.5 9.6 %fusion.35 = f32[128,96,2,64]{0,1,3,2:T(8,128)} fusion(f32[96,2,128,64]{2,0,3,1:T(8,128)} %copy.44), kind=kOutput, calls=%fused_computation.67 | convolution fusion | flops 2416164864 | bytes 12582912 | tf_op jit(solution)/shard_map/...ab,ac->...cb/dot_general | solution.py:24
  349.2 12.8 %subtract_bitcast_fusion.1 = (f32[96,2,128,64]{2,0,3,1:T(8,128)}, f32[96,2,128,64]{2,0,3,1:T(8,128)S(1)}) fusion(f32[128,64]{0,1:T(8,128)S(1)} %get-tuple-element.22, f32[128,64]{0,1:T(8,128)S(1)} %get-tuple-element.23, f32[128,96,2,64]{0,1,3,2:T(8,128)} %fusion.35, f32[128,96,2,64]{0,1,3,2:T(8,128)} %fusion.41, f32[128,96,2,64]{0,1,3,2:T(8,128)} %fusion.37, ...), kind=kOutput, calls=%fused_computation.6 | convolution fusion | flops 2428731392 | bytes 37814272 | tf_op jit(solution)/shard_map/...ab,ac->...cb/dot_general | solution.py:23
  361.9 10.0 %fusion.2 = f32[96,2,128,64]{2,3,1,0:T(8,128)S(1)} fusion(f32[96,2,128,64]{2,0,3,1:T(8,128)S(1)} %get-tuple-element.3), kind=kOutput, calls=%fused_computation.11 | convolution fusion | flops 1208020992 | bytes 12582912 | tf_op jit(solution)/shard_map/...cb,bd->...cd/dot_general | solution.py:26
  372.0 10.4 %fusion = f32[96,2,128,64]{2,3,1,0:T(8,128)S(1)} fusion(f32[96,2,128,64]{2,0,3,1:T(8,128)S(1)} %get-tuple-element.3), kind=kOutput, calls=%fused_computation.9 | convolution fusion | flops 1208016896 | bytes 12582912 | tf_op jit(solution)/shard_map/...cb,bd->...cd/dot_general | solution.py:25
  382.4 9.9 %subtract_bitcast_fusion = f32[1,96,2,128,64]{3,4,2,1,0:T(8,128)S(1)} fusion(f32[96,2,128,64]{2,3,1,0:T(8,128)S(1)} %fusion.2, f32[96,2,128,64]{2,0,3,1:T(8,128)S(1)} %bitcast.141), kind=kOutput, calls=%fused_computation.4 | convolution fusion | flops 1209589760 | bytes 18874368 | tf_op jit(solution)/shard_map/...cb,bd->...cd/dot_general | solution.py:23
  392.4 10.2 %add_bitcast_fusion = f32[1,96,2,128,64]{3,4,2,1,0:T(8,128)S(1)} fusion(f32[96,2,128,64]{2,3,1,0:T(8,128)S(1)} %fusion, f32[96,2,128,64]{2,0,3,1:T(8,128)S(1)} %bitcast.141), kind=kOutput, calls=%fused_computation.3 | convolution fusion | flops 1209593856 | bytes 18874368 | tf_op jit(solution)/shard_map/...cb,bd->...cd/dot_general | solution.py:24
  402.6 5.1 multiply_add_fusion.3
  407.7 4.8 pad_maximum_fusion.3
  412.5 0.1 fusion.126
  412.6 1.2 fusion.78
  413.9 123.7 %all-reduce.2.cloned.1.call-done = f32[2,32,2,128,64]{3,4,2,1,0:T(8,128)} async-done(((f32[2,32,2,128,64]{3,4,2,1,0:T(8,128)}), f32[2,32,2,128,64]{3,4,2,1,0:T(8,128)}) %all-reduce.2.cloned.1.call-update) | async-done | bytes 4194320 | tf_op jit(solution)/shard_map/psum | solution.py:135
  537.6 3.3 pad_maximum_fusion.1
  540.9 4.5 fusion.9
  545.4 4.1 fusion.8
  549.5 4.5 fusion.20
  554.0 4.6 fusion.21
  558.6 3.7 fusion.23
  562.3 5.5 fusion.22
  567.8 5.6 subtract_bitcast_fusion.3
  573.5 7.0 copy.52
  580.4 7.9 reshape.255
  588.3 8.4 add_bitcast_fusion.3
  596.7 6.9 copy.53
  603.6 7.9 reshape.256
  611.5 4.6 multiply_subtract_fusion
  616.1 3.8 pad_maximum_fusion.2
  619.9 20.3 %copy.54 = f32[2,64,2,8192]{1,2,0,3:T(2,128)} copy(f32[2,64,2,8192]{3,1,2,0:T(8,128)} %pad_maximum_fusion.2) | data formatting | bytes 16777216 | tf_op jit(solution)/shard_map/stack | solution.py:77
  640.2 22.3 %reshape.269 = f32[64,1,32768]{2,1,0:T(1,128)} reshape(f32[8192,2,2,64]{3,2,1,0:T(2,128)} %bitcast.138) | data formatting | bytes 16777216
  662.5 104.8 %all_to_all.44 = f32[64,1,32768]{2,1,0:T(1,128)} all-to-all(f32[64,1,32768]{2,1,0:T(1,128)} %reshape.269), channel_id=1, replica_groups=mesh['seq'=64,'dp'=2] {'seq'}, dimensions={0} | all-to-all | bytes 16777216 | tf_op jit(solution)/shard_map/all_to_all | solution.py:138
  767.4 0.5 broadcast.464
  767.9 25.2 %reduce = f32[64,32768]{1,0:T(8,128)} reduce(f32[64,1,32768]{2,1,0:T(1,128)} %all_to_all.44, f32[]{:T(128)} %broadcast.464), dimensions={1}, to_apply=%all_to_all.36.reduce_sub_computation | reduce | bytes 16777220 | tf_op jit(solution)/shard_map/all_to_all | solution.py:138
  793.1 16.4 %reshape.270 = f32[8192,2,2,64]{3,2,1,0:T(2,128)} reshape(f32[64,32768]{1,0:T(8,128)} %reduce) | data formatting | bytes 16777216
  809.4 23.2 %copy.55 = f32[2,64,2,64,128]{4,2,3,1,0:T(2,128)} copy(f32[2,64,2,64,128]{1,2,0,4,3:T(2,128)} %bitcast.139) | data formatting | bytes 16777216 | tf_op jit(solution)/shard_map/all_to_all | solution.py:138
  832.7 6.2 fusion.216
  838.9 4.3 fusion.74
  843.2 2.6 multiply_bitcast_fusion
  845.8 1.2 copy.56
  847.0 35.9 %all_to_all.45 = f32[64,64,128]{2,0,1:T(8,128)S(1)} all-to-all(f32[64,64,128]{2,0,1:T(8,128)S(1)} %copy.56), channel_id=1, replica_groups=mesh['seq'=64,'dp'=2] {'seq'}, dimensions={1} | all-to-all | bytes 4194304 | tf_op jit(solution)/shard_map/all_to_all | solution.py:140
  882.9 1.2 slice_bitcast_fusion.10
  884.1 0.6 copy.57
  884.7 0.2 reshape.257
  884.9 2.3 copy.88
  887.2 1.1 multiply_add_fusion.6
  (25 shorter events, 0.1 us)
Async XLA Ops:
  7.2 2.9 copy-start.6
  14.2 51.1 %all-to-all-start = ((f32[96,64,128]{2,0,1:T(8,128)}), f32[96,64,128]{2,0,1:T(8,128)S(1)}, u32[]{:S(2)}, u32[]{:S(2)}) async-start(f32[96,64,128]{2,0,1:T(8,128)} %copy.39), calls=%async_computation | async-start | bytes 6291456 | tf_op jit(solution)/shard_map/all_to_all | solution.py:128
  112.4 167.4 %all-to-all-start.1 = ((f32[2,96,128,128]{3,1,0,2:T(8,128)}), f32[2,96,128,128]{3,1,0,2:T(8,128)}, u32[]{:S(2)}, u32[]{:S(2)}) async-start(f32[2,96,128,128]{3,1,0,2:T(8,128)} %copy.42), calls=%async_computation.1 | async-start | bytes 25165824 | tf_op jit(solution)/shard_map/all_to_all | solution.py:129
  119.4 418.2 %all-reduce.2.cloned.1.call-start = ((), (), s32[]{:S(2)}) async-start(), calls=%async_computation.4 | async-start | bytes 8388608 | tf_op jit(solution)/shard_map/psum | solution.py:135
  314.1 9.6 %copy-start.3 = (f32[96,2,128,64]{2,0,3,1:T(8,128)S(1)}, f32[96,2,128,64]{2,0,3,1:T(8,128)}, u32[]{:S(2)}) copy-start(f32[96,2,128,64]{2,0,3,1:T(8,128)} %copy.45) | copy-start | bytes 18874372
  339.5 9.6 %copy-start.2 = (f32[96,2,128,64]{2,0,3,1:T(8,128)S(1)}, f32[96,2,128,64]{2,0,3,1:T(8,128)}, u32[]{:S(2)}) copy-start(f32[96,2,128,64]{2,0,3,1:T(8,128)} %copy.44) | copy-start | bytes 18874372
  361.9 20.4 %slice-start = ((s8[6291456]{0:T(1024)(128)(4,1)}), s8[4194304]{0:T(1024)(128)(4,1)S(1)}, s32[]{:S(2)}) async-start(s8[6291456]{0:T(1024)(128)(4,1)} %bitcast.140), calls=%async_computation.5 | async-start | bytes 8388608
  372.0 10.4 %slice-start.1 = ((s8[6291456]{0:T(1024)(128)(4,1)}), s8[2097152]{0:T(1024)(128)(4,1)S(1)}, s32[]{:S(2)}) async-start(s8[6291456]{0:T(1024)(128)(4,1)} %bitcast.140), calls=%async_computation.6 | async-start | bytes 4194304
  412.4 125.1 %copy-start.4 = (f32[1,32,2,128,64]{3,4,2,1,0:T(8,128)S(1)}, f32[1,32,2,128,64]{3,4,2,1,0:T(8,128)}, u32[]{:S(2)}) copy-start(f32[1,32,2,128,64]{3,4,2,1,0:T(8,128)} %get-tuple-element.8) | copy-start | bytes 6291460
  554.0 13.8 %copy-start = (f32[64,2,128,64]{2,3,1,0:T(8,128)}, f32[64,2,128,64]{2,3,1,0:T(8,128)S(1)}, u32[]{:S(2)}) copy-start(f32[64,2,128,64]{2,3,1,0:T(8,128)S(1)} %fusion.20) | copy-start | bytes 12582916
  558.6 9.2 %copy-start.1 = (f32[64,2,128,64]{2,3,1,0:T(8,128)}, f32[64,2,128,64]{2,3,1,0:T(8,128)S(1)}, u32[]{:S(2)}) copy-start(f32[64,2,128,64]{2,3,1,0:T(8,128)S(1)} %fusion.21) | copy-start | bytes 12582916
  884.1 3.1 copy-start.5
  884.1 3.1 copy-start.7
Sparse Core Ops, SparseCore 0:
  412.6 124.9 all-reduce.1
where the time goes:
time: 902 us; the launch traced here: 896 us
  waiting for transfers between devices  324 us (36%)
  local copies, waits for them, and re-layouts  190 us (21%)
  matrix products  147 us (16%)
  blocking collectives  141 us (16%)
  other arithmetic  61.5 us (7%)
  starting transfers between devices  18.2 us (2%)
  between operations  14.8 us (2%)
    all_to_all x1, waiting for transfers between devices, shards(): lax.all_to_all(mixed, 'seq', split_axis=2, concat_axis=3, tiled=True)  160 us
    psum x1, waiting for transfers between devices, shards(): filter_cross = lax.psum(filter_part, 'dp')  124 us
    all_to_all x1, blocking collectives, shards(): lax.all_to_all(turned, 'seq', split_axis=3, concat_axis=2, tiled=True)  105 us
    unnamed x26, local copies, waits for them, and re-layouts  43 us
    all_to_all x1, waiting for transfers between devices, shards(): lax.all_to_all(joined, 'seq', split_axis=1, concat_axis=1, tiled=True)  39.6 us
    all_to_all x1, blocking collectives, shards(): lax.all_to_all(back_rows, 'seq', split_axis=1, concat_axis=2, tiled=True)  35.9 us
    dot_general x4, matrix products, complex_section(): real_cos = jnp.einsum(form, real_part, cosines, precision=highest)  30.9 us
    dot_general x4, matrix products, complex_section(): imag_cos = jnp.einsum(form, imag_part, cosines, precision=highest)  30.8 us
  transfers between devices with their start and end apart: 3, of which 3 were waited for; matrix products, arithmetic and copies ran while one was open for 0% of the time, Pallas kernels for 0%

commit v1 on v0

v1 whole, which is shorter than its diff:
```python
import functools
import math

import jax
import jax.numpy as jnp
import ml_dtypes
import numpy as np
from jax import lax
from jax.experimental import pallas as pl
from jax.experimental.pallas import tpu as pltpu
from jax.sharding import PartitionSpec as P

MESH = pl.DeviceIdType.MESH
CHIPS = 32
ROWS = 16
COLS = 512
RAD = 128
LENGTH = CHIPS * 2 * ROWS * COLS
WIDE = 256


def two_parts(matrix):
    high = matrix.astype(ml_dtypes.bfloat16)
    low = (matrix - high.astype(np.float64)).astype(ml_dtypes.bfloat16)
    return high, low


def left_blocks(matrix):
    high, low = two_parts(matrix)
    return np.concatenate([high, low, high], axis=-1)


def right_blocks(matrix):
    high, low = two_parts(matrix)
    return np.concatenate([high, low, high], axis=-2)


@functools.cache
def tables():
    core = np.arange(2)[:, None, None, None]
    branch = np.arange(4)[None, :, None, None]
    freq = 8 * np.arange(RAD)[None, None, :, None] + core + 2 * branch
    row = np.arange(RAD)[None, None, None, :]
    angle = -2.0 * math.pi / 4096.0 * ((4 * freq + 1) * row % 4096)
    cos, sin = np.cos(angle), np.sin(angle)
    rows = np.concatenate([np.concatenate([cos, -sin], -1), np.concatenate([sin, cos], -1)], -2)
    scale = 1.0 / (LENGTH * math.sqrt(LENGTH))
    rows_back = np.swapaxes(rows, -1, -2) * scale
    column = np.arange(COLS)[None, None, None, :]
    angle = -2.0 * math.pi / (4 * LENGTH) * ((4 * freq + 1) * column % (4 * LENGTH))
    twiddle = np.stack([np.cos(angle), np.sin(angle)], axis=1).astype(np.float32)
    inner = np.arange(RAD)[None, :, None]
    outer = 4 * np.arange(RAD)[None, None, :] + np.arange(4)[:, None, None]
    angle = -2.0 * math.pi / COLS * (outer * inner % COLS)
    cos, sin = np.cos(angle), np.sin(angle)
    lanes = np.concatenate([np.concatenate([cos, sin], -1), np.concatenate([-sin, cos], -1)], -2)
    lanes_back = np.swapaxes(lanes, -1, -2)
    return (
        left_blocks(rows),
        left_blocks(rows_back),
        twiddle.reshape(2, 2, 4 * RAD, COLS),
        right_blocks(lanes),
        right_blocks(lanes_back),
    )


def split(value):
    high = value.astype(jnp.bfloat16)
    low = (value - high.astype(jnp.float32)).astype(jnp.bfloat16)
    return high, low


def butterfly(parts, sign):
    (ar, ai), (br, bi), (cr, ci), (dr, di) = parts
    pr, pi, mr, mi = ar + cr, ai + ci, ar - cr, ai - ci
    qr, qi, nr, ni = br + dr, bi + di, br - dr, bi - di
    first = (mr - sign * ni, mi + sign * nr)
    third = (mr + sign * ni, mi - sign * nr)
    return [(pr + qr, pi + qi), first, (pr - qr, pi - qi), third]


def turns(core):
    out = []
    for j in range(8):
        a = -2.0 * math.pi * j * 0.25 / 8.0
        b = -2.0 * math.pi * j * 1.25 / 8.0
        even = core == 0
        out.append(
            (
                jnp.where(even, jnp.float32(math.cos(a)), jnp.float32(math.cos(b))),
                jnp.where(even, jnp.float32(math.sin(a)), jnp.float32(math.sin(b))),
            )
        )
    return out


def dot(left, right):
    return lax.dot_general(left, right, (((1,), (0,)), ((), ())), preferred_element_type=jnp.float32)


def forward(core, x, rows, twiddle, lanes, work, spec):
    factors = turns(core)

    def columns(step, carry):
        cols = pl.ds(pl.multiple_of(step * WIDE, WIDE), WIDE)
        real = [x[4 * j : 4 * j + 4, :, :, cols].reshape(RAD, WIDE) for j in range(8)]
        parts = []
        for j in range(4):
            (ar, ai), (br, bi) = factors[j], factors[j + 4]
            parts.append((ar * real[j] + br * real[j + 4], ai * real[j] + bi * real[j + 4]))
        for branch, (re, im) in enumerate(butterfly(parts, -1.0)):
            high, low = split(jnp.concatenate([re, im], axis=0))
            out = dot(rows[branch], jnp.concatenate([high, high, low], axis=0))
            re, im = out[:RAD], out[RAD:]
            at = slice(branch * RAD, (branch + 1) * RAD)
            cos, sin = twiddle[0, at, cols], twiddle[1, at, cols]
            work[0, at, cols] = re * cos - im * sin
            work[1, at, cols] = re * sin + im * cos
        return carry

    lax.fori_loop(0, COLS // WIDE, columns, 0)

    def bands(step, carry):
        at = pl.ds(pl.multiple_of(step * RAD, RAD), RAD)
        parts = [(work[0, at, RAD * j : RAD * (j + 1)], work[1, at, RAD * j : RAD * (j + 1)]) for j in range(4)]
        for branch, (re, im) in enumerate(butterfly(parts, -1.0)):
            high, low = split(jnp.concatenate([re, im], axis=1))
            spec[branch, at, :] = dot(jnp.concatenate([high, high, low], axis=1), lanes[branch])
        return carry

    lax.fori_loop(0, 4, bands, 0)


def backward(core, left, right, rows_back, twiddle, lanes_back, wide, out):
    factors = turns(core)

    def bands(step, carry):
        at = pl.ds(pl.multiple_of(step * RAD, RAD), RAD)
        parts = []
        for branch in range(4):
            lr, li = left[branch, at, :RAD], left[branch, at, RAD:]
            rr, ri = right[branch, at, :RAD], right[branch, at, RAD:]
            high, low = split(jnp.concatenate([lr * rr + li * ri, li * rr - lr * ri], axis=1))
            back = dot(jnp.concatenate([high, high, low], axis=1), lanes_back[branch])
            parts.append((back[:, :RAD], back[:, RAD:]))
        for j, (re, im) in enumerate(butterfly(parts, 1.0)):
            cols = slice(RAD * j, RAD * (j + 1))
            cos, sin = twiddle[0, at, cols], twiddle[1, at, cols]
            high, low = split(jnp.concatenate([re * cos + im * sin, im * cos - re * sin], axis=0))
            wide[step, 0, :, cols] = high
            wide[step, 1, :, cols] = low
        return carry

    lax.fori_loop(0, 4, bands, 0)

    def columns(step, carry):
        cols = pl.ds(pl.multiple_of(step * WIDE, WIDE), WIDE)
        parts = []
        for branch in range(4):
            high, low = wide[branch, 0, :, cols], wide[branch, 1, :, cols]
            back = dot(rows_back[branch], jnp.concatenate([high, high, low], axis=0))
            parts.append((back[:RAD], back[RAD:]))
        sums = butterfly(parts, 1.0)
        for j in range(8):
            re, im = sums[j % 4]
            value = factors[j][0] * re + factors[j][1] * im
            out[4 * j : 4 * j + 4, :, :, cols] = value.reshape(4, 2, ROWS, WIDE)
        return carry

    lax.fori_loop(0, COLS // WIDE, columns, 0)


def kernel(
    grad, inputs, filters, rows_all, rows_back_all, twiddle_all, lanes_all, lanes_back_all,
    grad_out, filter_out,
    x, spec, work, wide, part, near, total, far, rows, rows_back, twiddle, lanes, lanes_back,
    table_sem, own_sem, send_sem, recv_sem, pass_send, pass_recv, part_send, part_recv,
    far_send, far_recv, out_send, out_recv, out_own,
):
    me, group = lax.axis_index("seq"), lax.axis_index("dp")
    core, chip = lax.rem(me, 2), me // 2
    side = lax.rem(chip // 4, 2)
    sibling = {"seq": chip * 2 + 1 - core}
    partner = {"dp": 1 - group}
    signals = (grad, inputs, filters)

    def remote(src, dst, send, recv, device):
        return pltpu.make_async_remote_copy(
            src_ref=src, dst_ref=dst, send_sem=send, recv_sem=recv, device_id=device, device_id_type=MESH
        )

    loads = [
        pltpu.make_async_copy(rows_all.at[core], rows, table_sem.at[0]),
        pltpu.make_async_copy(rows_back_all.at[core], rows_back, table_sem.at[1]),
        pltpu.make_async_copy(twiddle_all.at[core], twiddle, table_sem.at[2]),
        pltpu.make_async_copy(lanes_all, lanes, table_sem.at[3]),
        pltpu.make_async_copy(lanes_back_all, lanes_back, table_sem.at[4]),
    ]
    for load in loads:
        load.start()
    owns = [pltpu.make_async_copy(signals[q].at[chip], x.at[q, chip, core], own_sem.at[q]) for q in range(3)]
    for own in owns:
        own.start()

    barrier = pltpu.get_barrier_semaphore()

    def greet(step, carry):
        other = jnp.bitwise_xor(chip, step) * 2 + core
        pl.semaphore_signal(barrier, inc=1, device_id={"seq": other}, device_id_type=MESH)
        return carry

    def greet_far(step, carry):
        other = jnp.bitwise_xor(chip, step) * 2 + core
        pl.semaphore_signal(barrier, inc=1, device_id={"dp": 1 - group, "seq": other}, device_id_type=MESH)
        return carry

    lax.fori_loop(1, CHIPS, greet, 0)
    lax.fori_loop(0, CHIPS, greet_far, 0)
    pl.semaphore_signal(barrier, inc=1, device_id=sibling, device_id_type=MESH)
    pl.semaphore_wait(barrier, 2 * CHIPS)

    for q in range(3):

        def scatter(step, carry, q=q):
            other = jnp.bitwise_xor(chip, step)
            remote(
                signals[q].at[other], x.at[q, chip, core], send_sem.at[q], recv_sem.at[q], {"seq": other * 2 + core}
            ).start()
            return carry

        lax.fori_loop(1, CHIPS, scatter, 0)

    def all_but_own(q, sem):
        ref = x.at[q, pl.ds(0, CHIPS - 1), 0]
        return pltpu.make_async_copy(ref, ref, sem)

    def passing(q):
        half = x.at[q, :, core]
        return remote(half, half, pass_send.at[q], pass_recv.at[q], sibling)

    def arrive(q):
        owns[q].wait()
        all_but_own(q, recv_sem.at[q]).wait()
        passing(q).start()

    def exchange(k):
        return remote(part.at[k, :, 1 - core], near.at[k], part_send.at[k], part_recv.at[k], sibling)

    def reduce(k):
        exchange(k).wait_recv()
        for j in range(8):
            total[k, j // 2, j % 2] = part[k, 4 * j : 4 * j + 4, core] + near[k, 4 * j : 4 * j + 4]

    far_copy = remote(total.at[1, :, 1 - group], far, far_send, far_recv, partner)

    arrive(0)
    for load in loads:
        load.wait()
    passing(0).wait_recv()
    forward(core, x.at[0], rows, twiddle, lanes, work, spec.at[0])
    arrive(1)
    passing(1).wait_recv()
    forward(core, x.at[1], rows, twiddle, lanes, work, spec.at[1])
    backward(core, spec.at[0], spec.at[1], rows_back, twiddle, lanes_back, wide, part.at[1])
    exchange(1).start()
    reduce(1)
    far_copy.start()
    arrive(2)
    far_copy.wait_recv()
    for j in range(4):
        total[1, j, group] = total[1, j, group] + far[j]

    def filter_block(step):
        other = (step // 4) * 8 + group * 4 + lax.rem(step, 4)
        return other, total.at[1, step // 4, group, lax.rem(step, 4)]

    def filter_near(step, carry):
        other, block = filter_block(step)

        @pl.when(other != chip)
        def _():
            remote(block, filter_out.at[chip], out_send.at[1], out_recv.at[1], {"seq": other * 2 + core}).start()

        @pl.when(other == chip)
        def _():
            pltpu.make_async_copy(block, filter_out.at[chip], out_own.at[1]).start()

        return carry

    def filter_far(step, carry):
        other, block = filter_block(step)
        remote(
            block, filter_out.at[chip], out_send.at[2], out_recv.at[1], {"dp": 1 - group, "seq": other * 2 + core}
        ).start()
        return carry

    lax.fori_loop(0, CHIPS // 2, filter_near, 0)
    lax.fori_loop(0, CHIPS // 2, filter_far, 0)
    passing(2).wait_recv()
    forward(core, x.at[2], rows, twiddle, lanes, work, spec.at[2])
    backward(core, spec.at[0], spec.at[2], rows_back, twiddle, lanes_back, wide, part.at[0])
    exchange(0).start()
    reduce(0)

    def gradient(step, carry):
        other = jnp.bitwise_xor(chip, step)
        block = total.at[0, other // 8, lax.rem(other // 4, 2), lax.rem(other, 4)]
        remote(block, grad_out.at[chip], out_send.at[0], out_recv.at[0], {"seq": other * 2 + core}).start()
        return carry

    lax.fori_loop(1, CHIPS, gradient, 0)
    mine = total.at[0, chip // 8, side, lax.rem(chip, 4)]
    own_grad = pltpu.make_async_copy(mine, grad_out.at[chip], out_own.at[0])
    own_grad.start()

    def wait_blocks(count, sem):
        ref = x.at[0, pl.ds(0, count), 0]
        pltpu.make_async_copy(ref, ref, sem).wait()

    for q in range(3):
        all_but_own(q, send_sem.at[q]).wait()
        passing(q).wait_send()
    for k in range(2):
        exchange(k).wait_send()
    far_copy.wait_send()
    own_grad.wait()
    wait_blocks(CHIPS - 1, out_send.at[0])
    wait_blocks(CHIPS // 2, out_send.at[2])

    @pl.when(side == group)
    def _():
        wait_blocks(CHIPS // 2 - 1, out_send.at[1])
        wait_blocks(CHIPS - 1, out_recv.at[1])
        pltpu.make_async_copy(mine, filter_out.at[chip], out_own.at[1]).wait()

    @pl.when(side != group)
    def _():
        wait_blocks(CHIPS // 2, out_send.at[1])
        wait_blocks(CHIPS, out_recv.at[1])

    wait_blocks(CHIPS - 1, out_recv.at[0])


def shards(inputs, grad_out, filters, skip):
    channels = filters.shape[0]
    length = filters.shape[1]
    shape = (channels, ROWS, COLS)
    constants = tables()
    vmem, dma = pltpu.VMEM, pltpu.SemaphoreType.DMA
    any_space = pl.BlockSpec(memory_space=pl.ANY)
    conv, filter_grad = pl.pallas_call(
        kernel,
        out_shape=[jax.ShapeDtypeStruct(shape, jnp.float32)] * 2,
        in_specs=[any_space] * 8,
        out_specs=[pl.BlockSpec(memory_space=pltpu.VMEM)] * 2,
        scratch_shapes=[
            vmem((3, CHIPS, 2, ROWS, COLS), jnp.float32),
            vmem((3, 4, 4 * RAD, 2 * RAD), jnp.float32),
            vmem((2, 4 * RAD, COLS), jnp.float32),
            vmem((4, 2, 2 * RAD, COLS), jnp.bfloat16),
            vmem((2, CHIPS, 2, ROWS, COLS), jnp.float32),
            vmem((2, CHIPS, ROWS, COLS), jnp.float32),
            vmem((2, 4, 2, 4, ROWS, COLS), jnp.float32),
            vmem((4, 4, ROWS, COLS), jnp.float32),
            vmem(constants[0].shape[1:], jnp.bfloat16),
            vmem(constants[1].shape[1:], jnp.bfloat16),
            vmem(constants[2].shape[1:], jnp.float32),
            vmem(constants[3].shape, jnp.bfloat16),
            vmem(constants[4].shape, jnp.bfloat16),
            dma((5,)), dma((3,)), dma((3,)), dma((3,)), dma((3,)), dma((3,)), dma((2,)), dma((2,)),
            dma(()), dma(()), dma((3,)), dma((2,)), dma((2,)),
        ],
        compiler_params=pltpu.CompilerParams(
            collective_id=0, has_side_effects=True, vmem_limit_bytes=56 * 2**20
        ),
        cost_estimate=pl.CostEstimate(flops=9 * 10**9, bytes_accessed=2 * 10**7, transcendentals=0),
    )(
        grad_out.reshape(shape), inputs.reshape(shape), filters.reshape(shape),
        *(jnp.asarray(table) for table in constants),
    )
    grad_in = conv.reshape(1, channels, length) + skip[None, :, None] * grad_out
    return (grad_in, filter_grad.reshape(channels, length))


def solution(mesh):
    return jax.shard_map(
        shards,
        mesh=mesh,
        in_specs=(P("dp", None, "seq"), P("dp", None, "seq"), P(None, "seq"), P()),
        out_specs=(P("dp", None, "seq"), P(None, "seq")),
        check_vma=False,
    )
```

time: 902 us -> 130 us (0.14)
  the two profiles are of different devices: /device:TPU:1 before, /device:TPU:29 now
where the time goes in v1:
time: 130 us
  Pallas kernels  117 us (90%)
  local copies, waits for them, and re-layouts  10.4 us (8%)
    pallas_call x1, Pallas kernels, shards(): pl.pallas_call(kernel, out_shape=[jax.ShapeDtypeStruct(shape, jnp.float32...  117 us
    unnamed x10, local copies, waits for them, and re-layouts  8.87 us

profile of v1, /device:TPU:29, one launch (start us, length us, event | category | flops | bytes accessed | tf_op | source)
XLA Modules:
  0.0 129.6 jit_solution(3532352537731782252)
XLA Ops:
  0.6 0.0 copy-start
  0.6 2.9 %copy.12 = f32[4,8,16,512]{3,2,1,0:T(8,128)} copy(f32[4,8,16,512]{3,1,2,0:T(8,128)} %bitcast.11) | data formatting | bytes 2097152
  3.5 2.8 %copy.13 = f32[4,8,16,512]{3,2,1,0:T(8,128)} copy(f32[4,8,16,512]{3,1,2,0:T(8,128)} %bitcast.12) | data formatting | bytes 2097152
  6.3 0.0 copy-done
  6.3 1.6 %copy.11 = f32[4,8,16,512]{3,2,1,0:T(8,128)} copy(f32[4,8,16,512]{3,1,2,0:T(8,128)S(1)} %bitcast.10) | data formatting | bytes 2097152
  7.9 0.0 copy-start.2
  7.9 117.5 %shard_map.104 = (f32[32,16,512]{2,1,0:T(8,128)}, f32[32,16,512]{2,1,0:T(8,128)}) custom-call(f32[32,16,512]{2,1,0:T(8,128)} %bitcast.16, f32[32,16,512]{2,1,0:T(8,128)} %bitcast.14, f32[32,16,512]{2,1,0:T(8,128)} %bitcast.15, bf16[2,4,256,768]{3,2,1,0:T(8,128)(2,1)} %constant.10.clone.rows_all, bf16[2,4,256,768]{3,2,1,0:T(8,128)(2,1)} %constant.11.clone.rows_back_all, ...), custom_call_target="tpu_custom_call" | custom-call | flops 8999999488 | bytes 20000000 | tf_op jit(solution)/shard_map/pallas_call | solution.py:351
  125.4 0.0 copy-start.1
  125.4 1.5 %reshape.25 = f32[1,32,8192]{2,1,0:T(8,128)S(1)} reshape(f32[32,16,512]{2,1,0:T(8,128)} %get-tuple-element.4) | data formatting | bytes 2097152 | tf_op jit(solution)/shard_map/reshape | solution.py:381
  126.9 0.0 copy-done.2
  126.9 1.1 multiply_add_fusion
  128.0 0.0 copy-done.1
  128.0 1.6 %copy.14 = f32[4,8,16,512]{3,1,2,0:T(8,128)} copy(f32[4,8,16,512]{3,2,1,0:T(8,128)S(1)} %bitcast.13) | data formatting | bytes 2097152
Async XLA Ops:
  0.6 5.7 %copy-start = (f32[1,32,8192]{2,1,0:T(8,128)S(1)}, f32[1,32,8192]{2,1,0:T(8,128)}, u32[]{:S(2)}) copy-start(f32[1,32,8192]{2,1,0:T(8,128)} %param.10) | copy-start | bytes 3145732
  7.9 119.0 %copy-start.2 = (f32[32]{0:T(128)S(1)}, f32[32]{0:T(128)}, u32[]{:S(2)}) copy-start(f32[32]{0:T(128)} %param.12) | copy-start | bytes 388
  125.4 2.7 %copy-start.1 = (f32[32,16,512]{2,1,0:T(8,128)S(1)}, f32[32,16,512]{2,1,0:T(8,128)}, u32[]{:S(2)}) copy-start(f32[32,16,512]{2,1,0:T(8,128)} %get-tuple-element.5) | copy-start | bytes 3145732

commit v2 on v1

--- a/solution.py
+++ b/solution.py
@@ -171,36 +171,38 @@
 
 
 def kernel(
-    grad, inputs, filters, rows_all, rows_back_all, twiddle_all, lanes_all, lanes_back_all,
-    grad_out, filter_out,
-    x, spec, work, wide, part, near, total, far, rows, rows_back, twiddle, lanes, lanes_back,
-    table_sem, own_sem, send_sem, recv_sem, pass_send, pass_recv, part_send, part_recv,
+    grad, filters, inputs, rows_all, rows_back_all, twiddle_all, lanes_all, lanes_back_all,
+    landed,
+    raw, rolled, x, spec, work, wide, part, near, total, far, rows, rows_back, twiddle, lanes, lanes_back,
+    table_sem, raw_sem, own_sem, send_sem, recv_sem, pass_send, pass_recv, part_send, part_recv,
     far_send, far_recv, out_send, out_recv, out_own,
 ):
     me, group = lax.axis_index("seq"), lax.axis_index("dp")
     core, chip = lax.rem(me, 2), me // 2
-    side = lax.rem(chip // 4, 2)
+    side = lax.rem(chip // 8 + chip, 2)
+    flip = 4 * group
+    channel = jnp.bitwise_xor(chip, flip)
     sibling = {"seq": chip * 2 + 1 - core}
-    partner = {"dp": 1 - group}
-    signals = (grad, inputs, filters)
+    partner = {"dp": 1 - group, "seq": jnp.bitwise_xor(chip, 4) * 2 + core}
+    signals = (grad, filters, inputs)
 
     def remote(src, dst, send, recv, device):
         return pltpu.make_async_remote_copy(
             src_ref=src, dst_ref=dst, send_sem=send, recv_sem=recv, device_id=device, device_id_type=MESH
         )
 
+    raws = [pltpu.make_async_copy(signals[q], raw.at[q], raw_sem.at[q]) for q in range(3)]
+    for copy in raws:
+        copy.start()
     loads = [
         pltpu.make_async_copy(rows_all.at[core], rows, table_sem.at[0]),
-        pltpu.make_async_copy(rows_back_all.at[core], rows_back, table_sem.at[1]),
-        pltpu.make_async_copy(twiddle_all.at[core], twiddle, table_sem.at[2]),
-        pltpu.make_async_copy(lanes_all, lanes, table_sem.at[3]),
-        pltpu.make_async_copy(lanes_back_all, lanes_back, table_sem.at[4]),
+        pltpu.make_async_copy(twiddle_all.at[core], twiddle, table_sem.at[1]),
+        pltpu.make_async_copy(lanes_all, lanes, table_sem.at[2]),
+        pltpu.make_async_copy(lanes_back_all, lanes_back, table_sem.at[3]),
+        pltpu.make_async_copy(rows_back_all.at[core], rows_back, table_sem.at[4]),
     ]
     for load in loads:
         load.start()
-    owns = [pltpu.make_async_copy(signals[q].at[chip], x.at[q, chip, core], own_sem.at[q]) for q in range(3)]
-    for own in owns:
-        own.start()
 
     barrier = pltpu.get_barrier_semaphore()
 
@@ -209,26 +211,27 @@
         pl.semaphore_signal(barrier, inc=1, device_id={"seq": other}, device_id_type=MESH)
         return carry
 
-    def greet_far(step, carry):
-        other = jnp.bitwise_xor(chip, step) * 2 + core
-        pl.semaphore_signal(barrier, inc=1, device_id={"dp": 1 - group, "seq": other}, device_id_type=MESH)
-        return carry
-
     lax.fori_loop(1, CHIPS, greet, 0)
-    lax.fori_loop(0, CHIPS, greet_far, 0)
-    pl.semaphore_signal(barrier, inc=1, device_id=sibling, device_id_type=MESH)
-    pl.semaphore_wait(barrier, 2 * CHIPS)
-
-    for q in range(3):
-
-        def scatter(step, carry, q=q):
+    for other in (sibling, partner):
+        pl.semaphore_signal(barrier, inc=1, device_id=other, device_id_type=MESH)
+
+    def roll(q):
+        raws[q].wait()
+        for n in range(ROWS):
+            rolled[q, :, n, :] = raw[q, :, n * COLS : (n + 1) * COLS]
+
+    def own(q):
+        return pltpu.make_async_copy(rolled.at[q, channel], x.at[q, chip, core], own_sem.at[q])
+
+    def scatter(q):
+        def one(step, carry):
             other = jnp.bitwise_xor(chip, step)
-            remote(
-                signals[q].at[other], x.at[q, chip, core], send_sem.at[q], recv_sem.at[q], {"seq": other * 2 + core}
-            ).start()
+            block = rolled.at[q, jnp.bitwise_xor(other, flip)]
+            remote(block, x.at[q, chip, core], send_sem.at[q], recv_sem.at[q], {"seq": other * 2 + core}).start()
             return carry
 
-        lax.fori_loop(1, CHIPS, scatter, 0)
+        lax.fori_loop(1, CHIPS, one, 0)
+        own(q).start()
 
     def all_but_own(q, sem):
         ref = x.at[q, pl.ds(0, CHIPS - 1), 0]
@@ -239,7 +242,7 @@
         return remote(half, half, pass_send.at[q], pass_recv.at[q], sibling)
 
     def arrive(q):
-        owns[q].wait()
+        own(q).wait()
         all_but_own(q, recv_sem.at[q]).wait()
         passing(q).start()
 
@@ -251,109 +254,140 @@
         for j in range(8):
             total[k, j // 2, j % 2] = part[k, 4 * j : 4 * j + 4, core] + near[k, 4 * j : 4 * j + 4]
 
-    far_copy = remote(total.at[1, :, 1 - group], far, far_send, far_recv, partner)
-
+    def place(owner, piece, i):
+        diagonal = owner + 2 * lax.rem(piece // 2 + channel // 8, 2)
+        return i, lax.rem(piece + channel // 4, 2), lax.rem(diagonal + 4 - i, 4)
+
+    def far_start(piece):
+        for i in range(4):
+            at = place(1 - group, piece, i)
+            remote(
+                total.at[1, at[0], at[1], at[2]], far.at[piece, i], far_send.at[piece], far_recv.at[piece], partner
+            ).start()
+
+    def far_wait(piece, sem):
+        ref = far.at[piece]
+        pltpu.make_async_copy(ref, ref, sem.at[piece]).wait()
+
+    roll(0)
+    pl.semaphore_wait(barrier, CHIPS + 1)
+    scatter(0)
+    roll(1)
+    roll(2)
+    all_but_own(0, send_sem.at[0]).wait()
+    scatter(1)
     arrive(0)
     for load in loads:
         load.wait()
     passing(0).wait_recv()
     forward(core, x.at[0], rows, twiddle, lanes, work, spec.at[0])
+    all_but_own(1, send_sem.at[1]).wait()
+    scatter(2)
     arrive(1)
     passing(1).wait_recv()
     forward(core, x.at[1], rows, twiddle, lanes, work, spec.at[1])
-    backward(core, spec.at[0], spec.at[1], rows_back, twiddle, lanes_back, wide, part.at[1])
-    exchange(1).start()
-    reduce(1)
-    far_copy.start()
-    arrive(2)
-    far_copy.wait_recv()
-    for j in range(4):
-        total[1, j, group] = total[1, j, group] + far[j]
-
-    def filter_block(step):
-        other = (step // 4) * 8 + group * 4 + lax.rem(step, 4)
-        return other, total.at[1, step // 4, group, lax.rem(step, 4)]
-
-    def filter_near(step, carry):
-        other, block = filter_block(step)
-
-        @pl.when(other != chip)
-        def _():
-            remote(block, filter_out.at[chip], out_send.at[1], out_recv.at[1], {"seq": other * 2 + core}).start()
-
-        @pl.when(other == chip)
-        def _():
-            pltpu.make_async_copy(block, filter_out.at[chip], out_own.at[1]).start()
-
-        return carry
-
-    def filter_far(step, carry):
-        other, block = filter_block(step)
-        remote(
-            block, filter_out.at[chip], out_send.at[2], out_recv.at[1], {"dp": 1 - group, "seq": other * 2 + core}
-        ).start()
-        return carry
-
-    lax.fori_loop(0, CHIPS // 2, filter_near, 0)
-    lax.fori_loop(0, CHIPS // 2, filter_far, 0)
-    passing(2).wait_recv()
-    forward(core, x.at[2], rows, twiddle, lanes, work, spec.at[2])
-    backward(core, spec.at[0], spec.at[2], rows_back, twiddle, lanes_back, wide, part.at[0])
+    backward(core, spec.at[0], spec.at[1], rows_back, twiddle, lanes_back, wide, part.at[0])
     exchange(0).start()
     reduce(0)
 
     def gradient(step, carry):
         other = jnp.bitwise_xor(chip, step)
         block = total.at[0, other // 8, lax.rem(other // 4, 2), lax.rem(other, 4)]
-        remote(block, grad_out.at[chip], out_send.at[0], out_recv.at[0], {"seq": other * 2 + core}).start()
-        return carry
-
+        remote(block, landed.at[0, channel], out_send.at[0], out_recv.at[0], {"seq": other * 2 + core}).start()
+        return carry
+
+    all_but_own(2, send_sem.at[2]).wait()
     lax.fori_loop(1, CHIPS, gradient, 0)
-    mine = total.at[0, chip // 8, side, lax.rem(chip, 4)]
-    own_grad = pltpu.make_async_copy(mine, grad_out.at[chip], out_own.at[0])
+    mine = [total.at[k, chip // 8, lax.rem(chip // 4, 2), lax.rem(chip, 4)] for k in range(2)]
+    own_grad = pltpu.make_async_copy(mine[0], landed.at[0, channel], out_own.at[0])
     own_grad.start()
+
+    arrive(2)
+    passing(2).wait_recv()
+    forward(core, x.at[2], rows, twiddle, lanes, work, spec.at[2])
+    backward(core, spec.at[0], spec.at[2], rows_back, twiddle, lanes_back, wide, part.at[1])
+    exchange(1).start()
+    reduce(1)
+    for piece in range(4):
+        far_start(piece)
+    for piece in range(4):
+        far_wait(piece, far_recv)
+
+        def settle(i, carry, piece=piece):
+            at = place(group, piece, i)
+            block = total.at[1, at[0], at[1], at[2]]
+            block[...] = block[...] + far[piece, i]
+            other = at[0] * 8 + at[1] * 4 + at[2]
+
+            @pl.when(other != chip)
+            def _():
+                remote(block, landed.at[1, channel], out_send.at[1], out_recv.at[1], {"seq": other * 2 + core}).start()
+
+            @pl.when(other == chip)
+            def _():
+                pltpu.make_async_copy(block, landed.at[1, channel], out_own.at[1]).start()
+
+            device = {"dp": 1 - group, "seq": other * 2 + core}
+            remote(block, landed.at[1, channel], out_send.at[2], out_recv.at[1], device).start()
+            return carry
+
+        lax.fori_loop(0, 4, settle, 0)
 
     def wait_blocks(count, sem):
         ref = x.at[0, pl.ds(0, count), 0]
         pltpu.make_async_copy(ref, ref, sem).wait()
 
     for q in range(3):
-        all_but_own(q, send_sem.at[q]).wait()
         passing(q).wait_send()
     for k in range(2):
         exchange(k).wait_send()
-    far_copy.wait_send()
-    own_grad.wait()
-    wait_blocks(CHIPS - 1, out_send.at[0])
-    wait_blocks(CHIPS // 2, out_send.at[2])
+    for piece in range(4):
+        far_wait(piece, far_send)
 
     @pl.when(side == group)
     def _():
         wait_blocks(CHIPS // 2 - 1, out_send.at[1])
         wait_blocks(CHIPS - 1, out_recv.at[1])
-        pltpu.make_async_copy(mine, filter_out.at[chip], out_own.at[1]).wait()
+        pltpu.make_async_copy(mine[1], landed.at[1, channel], out_own.at[1]).wait()
 
     @pl.when(side != group)
     def _():
         wait_blocks(CHIPS // 2, out_send.at[1])
         wait_blocks(CHIPS, out_recv.at[1])
 
+    wait_blocks(CHIPS // 2, out_send.at[2])
+    wait_blocks(CHIPS - 1, out_send.at[0])
+    own_grad.wait()
     wait_blocks(CHIPS - 1, out_recv.at[0])
 
 
+def finish(landed, grad, skip, grad_in, filter_grad):
+    channels = grad.shape[0]
+    shape = (channels, skip.shape[1])
+    chosen = lax.broadcasted_iota(jnp.int32, shape, 1) == (
+        lax.broadcasted_iota(jnp.int32, shape, 0) + pl.program_id(0) * channels
+    )
+    gain = jnp.sum(jnp.where(chosen, skip[...], 0.0), axis=1, keepdims=True)
+    for n in range(ROWS):
+        at = slice(n * COLS, (n + 1) * COLS)
+        grad_in[:, at] = landed[0, :, n, :] + gain * grad[:, at]
+        filter_grad[:, at] = landed[1, :, n, :]
+
+
 def shards(inputs, grad_out, filters, skip):
-    channels = filters.shape[0]
-    length = filters.shape[1]
-    shape = (channels, ROWS, COLS)
+    channels, length = filters.shape
     constants = tables()
     vmem, dma = pltpu.VMEM, pltpu.SemaphoreType.DMA
     any_space = pl.BlockSpec(memory_space=pl.ANY)
-    conv, filter_grad = pl.pallas_call(
+    grad = grad_out.reshape(channels, length)
+    landed = pl.pallas_call(
         kernel,
-        out_shape=[jax.ShapeDtypeStruct(shape, jnp.float32)] * 2,
+        out_shape=jax.ShapeDtypeStruct((2, CHIPS, ROWS, COLS), jnp.float32),
         in_specs=[any_space] * 8,
-        out_specs=[pl.BlockSpec(memory_space=pltpu.VMEM)] * 2,
+        out_specs=any_space,
         scratch_shapes=[
+            vmem((3, channels, length), jnp.float32),
+            vmem((3, CHIPS, ROWS, COLS), jnp.float32),
             vmem((3, CHIPS, 2, ROWS, COLS), jnp.float32),
             vmem((3, 4, 4 * RAD, 2 * RAD), jnp.float32),
             vmem((2, 4 * RAD, COLS), jnp.float32),
@@ -367,19 +401,31 @@
             vmem(constants[2].shape[1:], jnp.float32),
             vmem(constants[3].shape, jnp.bfloat16),
             vmem(constants[4].shape, jnp.bfloat16),
-            dma((5,)), dma((3,)), dma((3,)), dma((3,)), dma((3,)), dma((3,)), dma((2,)), dma((2,)),
-            dma(()), dma(()), dma((3,)), dma((2,)), dma((2,)),
+            dma((5,)), dma((3,)), dma((3,)), dma((3,)), dma((3,)), dma((3,)), dma((3,)), dma((2,)), dma((2,)),
+            dma((4,)), dma((4,)), dma((3,)), dma((2,)), dma((2,)),
         ],
         compiler_params=pltpu.CompilerParams(
             collective_id=0, has_side_effects=True, vmem_limit_bytes=56 * 2**20
         ),
         cost_estimate=pl.CostEstimate(flops=9 * 10**9, bytes_accessed=2 * 10**7, transcendentals=0),
     )(
-        grad_out.reshape(shape), inputs.reshape(shape), filters.reshape(shape),
+        grad, filters, inputs.reshape(channels, length),
         *(jnp.asarray(table) for table in constants),
     )
-    grad_in = conv.reshape(1, channels, length) + skip[None, :, None] * grad_out
-    return (grad_in, filter_grad.reshape(channels, length))
+    flat = pl.BlockSpec((8, length), lambda i: (i, 0))
+    grad_in, filter_grad = pl.pallas_call(
+        finish,
+        out_shape=[jax.ShapeDtypeStruct((channels, length), jnp.float32)] * 2,
+        grid=(channels // 8,),
+        in_specs=[
+            pl.BlockSpec((2, 8, ROWS, COLS), lambda i: (0, i, 0, 0)),
+            flat,
+            pl.BlockSpec((1, channels), lambda i: (0, 0)),
+        ],
+        out_specs=[flat, flat],
+        cost_estimate=pl.CostEstimate(flops=10**6, bytes_accessed=5 * 2**20, transcendentals=0),
+    )(landed, grad, skip.reshape(1, channels))
+    return (grad_in.reshape(1, channels, length), filter_grad)
 
 
 def solution(mesh):

time: 130 us -> 93.8 us (0.72)
  the two profiles are of different devices: /device:TPU:29 before, /device:TPU:24 now
where the time goes in v2:
time: 93.8 us; the launch traced here: 93.6 us
  Pallas kernels  93 us (99%)
    pallas_call x1, Pallas kernels, shards(): pl.pallas_call(kernel, out_shape=jax.ShapeDtypeStruct((2, CHIPS, ROWS, CO...  88.8 us
    pallas_call x1, Pallas kernels, shards(): pl.pallas_call(finish, out_shape=[jax.ShapeDtypeStruct((channels, length)...  4.13 us

profile of v2, /device:TPU:24, one launch (start us, length us, event | category | flops | bytes accessed | tf_op | source)
XLA Modules:
  0.0 93.6 jit_solution(1061697103012379491)
XLA Ops:
  0.6 88.8 %shard_map.104.landed = f32[2,32,16,512]{3,2,1,0:T(8,128)} custom-call(f32[32,8192]{1,0:T(8,128)} %bitcast.4, f32[32,8192]{1,0:T(8,128)} %filters.1, f32[32,8192]{1,0:T(8,128)} %bitcast.7, bf16[2,4,256,768]{3,2,1,0:T(8,128)(2,1)} %constant.10.clone.rows_all, bf16[2,4,256,768]{3,2,1,0:T(8,128)(2,1)} %constant.11.clone.rows_back_all, ...), custom_call_target="tpu_custom_call" | custom-call | flops 8999999488 | bytes 20000000 | tf_op jit(solution)/shard_map/pallas_call | solution.py:383
  89.5 4.1 %shard_map.105 = (f32[32,8192]{1,0:T(8,128)}, f32[32,8192]{1,0:T(8,128)}) custom-call(f32[2,32,16,512]{3,2,1,0:T(8,128)} %shard_map.104.landed, f32[32,8192]{1,0:T(8,128)} %bitcast.5, f32[1,32]{1,0:T(1,128)} %bitcast.6), custom_call_target="tpu_custom_call" | custom-call | flops 1000000 | bytes 5242880 | tf_op jit(solution)/shard_map/pallas_call | solution.py:416

commit v3 on v2

v3 whole, which is shorter than its diff:
```python
import functools
import math

import jax
import jax.numpy as jnp
import ml_dtypes
import numpy as np
from jax import lax
from jax.experimental import pallas as pl
from jax.experimental.pallas import tpu as pltpu
from jax.sharding import PartitionSpec as P

MESH = pl.DeviceIdType.MESH
CHIPS = 32
ROWS = 16
COLS = 512
RAD = 128
LENGTH = CHIPS * 2 * ROWS * COLS


def two_parts(matrix):
    high = matrix.astype(ml_dtypes.bfloat16)
    low = (matrix - high.astype(np.float64)).astype(ml_dtypes.bfloat16)
    return high, low


def left_blocks(matrix):
    high, low = two_parts(matrix)
    return np.concatenate([high, low, high], axis=-1)


def right_blocks(matrix):
    high, low = two_parts(matrix)
    return np.concatenate([high, low, high], axis=-2)


@functools.cache
def tables():
    core = np.arange(2)[:, None, None, None]
    branch = np.arange(4)[None, :, None, None]
    freq = 8 * np.arange(RAD)[None, None, :, None] + core + 2 * branch
    row = np.arange(RAD)[None, None, None, :]
    angle = -2.0 * math.pi / 4096.0 * ((4 * freq + 1) * row % 4096)
    cos, sin = np.cos(angle), np.sin(angle)
    rows = np.concatenate([np.concatenate([cos, -sin], -1), np.concatenate([sin, cos], -1)], -2)
    scale = 1.0 / (LENGTH * math.sqrt(LENGTH))
    rows_back = np.swapaxes(rows, -1, -2) * scale
    column = np.arange(COLS)[None, None, None, :]
    angle = -2.0 * math.pi / (4 * LENGTH) * ((4 * freq + 1) * column % (4 * LENGTH))
    twiddle = np.stack([np.cos(angle), np.sin(angle)], axis=1).astype(np.float32)
    inner = np.arange(RAD)[None, :, None]
    outer = 4 * np.arange(RAD)[None, None, :] + np.arange(4)[:, None, None]
    angle = -2.0 * math.pi / COLS * (outer * inner % COLS)
    cos, sin = np.cos(angle), np.sin(angle)
    lanes = np.concatenate([np.concatenate([cos, sin], -1), np.concatenate([-sin, cos], -1)], -2)
    lanes_back = np.swapaxes(lanes, -1, -2)
    return (
        left_blocks(rows),
        left_blocks(rows_back),
        twiddle.reshape(2, 2, 4 * RAD, COLS),
        right_blocks(lanes),
        right_blocks(lanes_back),
    )


def split(value):
    high = value.astype(jnp.bfloat16)
    low = (value - high.astype(jnp.float32)).astype(jnp.bfloat16)
    return high, low


def butterfly(parts, sign):
    (ar, ai), (br, bi), (cr, ci), (dr, di) = parts
    pr, pi, mr, mi = ar + cr, ai + ci, ar - cr, ai - ci
    qr, qi, nr, ni = br + dr, bi + di, br - dr, bi - di
    first = (mr - sign * ni, mi + sign * nr)
    third = (mr + sign * ni, mi - sign * nr)
    return [(pr + qr, pi + qi), first, (pr - qr, pi - qi), third]


def turns(half):
    angles = [-2.0 * math.pi * j * (half + 0.25) / 8.0 for j in range(8)]
    return [(math.cos(angle), math.sin(angle)) for angle in angles]


def dot(left, right):
    return lax.dot_general(left, right, (((1,), (0,)), ((), ())), preferred_element_type=jnp.float32)


def forward(x, rows, twiddle, lanes, work, spec):
    real = [x[4 * j : 4 * j + 4].reshape(RAD, COLS) for j in range(8)]
    for half in range(2):
        factors = turns(half)
        parts = []
        for j in range(4):
            (ar, ai), (br, bi) = factors[j], factors[j + 4]
            parts.append((ar * real[j] + br * real[j + 4], ai * real[j] + bi * real[j + 4]))
        for branch, (re, im) in enumerate(butterfly(parts, -1.0)):
            high, low = split(jnp.concatenate([re, im], axis=0))
            out = dot(rows[half, branch], jnp.concatenate([high, high, low], axis=0))
            re, im = out[:RAD], out[RAD:]
            at = slice(branch * RAD, (branch + 1) * RAD)
            cos, sin = twiddle[half, 0, at], twiddle[half, 1, at]
            work[half, 0, at] = re * cos - im * sin
            work[half, 1, at] = re * sin + im * cos

    def bands(half, carry):
        parts = [
            (work[half, 0, :, RAD * j : RAD * (j + 1)], work[half, 1, :, RAD * j : RAD * (j + 1)]) for j in range(4)
        ]
        for branch, (re, im) in enumerate(butterfly(parts, -1.0)):
            high, low = split(jnp.concatenate([re, im], axis=1))
            spec[half, branch] = dot(jnp.concatenate([high, high, low], axis=1), lanes[branch])
        return carry

    lax.fori_loop(0, 2, bands, 0)


def backward(left, right, rows_back, twiddle, lanes_back, wide, out):
    def bands(half, carry):
        parts = []
        for branch in range(4):
            lr, li = left[half, branch, :, :RAD], left[half, branch, :, RAD:]
            rr, ri = right[half, branch, :, :RAD], right[half, branch, :, RAD:]
            high, low = split(jnp.concatenate([lr * rr + li * ri, li * rr - lr * ri], axis=1))
            back = dot(jnp.concatenate([high, high, low], axis=1), lanes_back[branch])
            parts.append((back[:, :RAD], back[:, RAD:]))
        for j, (re, im) in enumerate(butterfly(parts, 1.0)):
            cols = slice(RAD * j, RAD * (j + 1))
            cos, sin = twiddle[half, 0, :, cols], twiddle[half, 1, :, cols]
            for side, value in enumerate((re * cos + im * sin, im * cos - re * sin)):
                high, low = split(value.reshape(4, RAD, RAD))
                wide[half, :, 0, side * RAD : (side + 1) * RAD, cols] = high
                wide[half, :, 1, side * RAD : (side + 1) * RAD, cols] = low
        return carry

    lax.fori_loop(0, 2, bands, 0)
    values = [0.0] * 8
    for half in range(2):
        factors = turns(half)
        parts = []
        for branch in range(4):
            high, low = wide[half, branch, 0], wide[half, branch, 1]
            back = dot(rows_back[half, branch], jnp.concatenate([high, high, low], axis=0))
            parts.append((back[:RAD], back[RAD:]))
        sums = butterfly(parts, 1.0)
        for j in range(8):
            re, im = sums[j % 4]
            values[j] = values[j] + (factors[j][0] * re + factors[j][1] * im)
    for j in range(8):
        out[4 * j : 4 * j + 4] = values[j].reshape(4, 2, ROWS, COLS)


def kernel(
    grad, inputs, filters, rows_all, rows_back_all, twiddle_all, lanes_all, lanes_back_all,
    landed,
    raw, rolled, x, spec, work, wide, part, far, rows, rows_back, twiddle, lanes, lanes_back,
    table_sem, raw_sem, own_sem, send_sem, recv_sem, pass_send, pass_recv, ready, far_send, far_recv,
    out_send, out_recv, out_own,
):
    me, group = lax.axis_index("seq"), lax.axis_index("dp")
    core, chip = lax.rem(me, 2), me // 2
    side = lax.rem(chip // 8 + chip, 2)
    flip = 4 * group
    channel = jnp.bitwise_xor(chip, flip)
    sibling = {"seq": chip * 2 + 1 - core}
    partner = {"dp": 1 - group, "seq": jnp.bitwise_xor(chip, 4) * 2 + core}
    signals = (grad, inputs, filters)
    bulk = rolled.reshape(3 * CHIPS, ROWS, COLS)
    goals = (core, 1, 0)

    def remote(src, dst, send, recv, device):
        return pltpu.make_async_remote_copy(
            src_ref=src, dst_ref=dst, send_sem=send, recv_sem=recv, device_id=device, device_id_type=MESH
        )

    raws = [pltpu.make_async_copy(signals[q], raw.at[q], raw_sem.at[q]) for q in range(3)]
    for copy in raws:
        copy.start()
    loads = [
        pltpu.make_async_copy(rows_all, rows, table_sem.at[0]),
        pltpu.make_async_copy(twiddle_all, twiddle, table_sem.at[1]),
        pltpu.make_async_copy(lanes_all, lanes, table_sem.at[2]),
        pltpu.make_async_copy(lanes_back_all, lanes_back, table_sem.at[3]),
        pltpu.make_async_copy(rows_back_all, rows_back, table_sem.at[4]),
    ]
    for load in loads:
        load.start()

    barrier = pltpu.get_barrier_semaphore()

    def greet(step, carry):
        other = jnp.bitwise_xor(chip, step) * 2 + core
        pl.semaphore_signal(barrier, inc=1, device_id={"seq": other}, device_id_type=MESH)
        return carry

    lax.fori_loop(1, CHIPS, greet, 0)
    for other in (sibling, partner):
        pl.semaphore_signal(barrier, inc=1, device_id=other, device_id_type=MESH)

    def roll(q):
        raws[q].wait()
        for n in range(ROWS):
            rolled[q, :, n, :] = raw[q, :, n * COLS : (n + 1) * COLS]

    def slot(q):
        return x.at[min(q, 1), chip, core]

    def own(q):
        return pltpu.make_async_copy(rolled.at[q, channel], slot(q), own_sem.at[q])

    def scatter(q):
        def one(step, carry):
            other = jnp.bitwise_xor(chip, step)
            block = rolled.at[q, jnp.bitwise_xor(other, flip)]
            device = {"seq": other * 2 + goals[q]}
            remote(block, slot(q), send_sem.at[q], recv_sem.at[min(q, 1)], device).start()
            return carry

        lax.fori_loop(1, CHIPS, one, 0)
        if q == 0:
            own(q).start()
            return

        @pl.when(core == goals[q])
        def _():
            own(q).start()

        @pl.when(core != goals[q])
        def _():
            remote(rolled.at[q, channel], slot(q), send_sem.at[q], recv_sem.at[1], sibling).start()

    def wait_blocks(count, sem):
        ref = bulk.at[pl.ds(0, count)]
        pltpu.make_async_copy(ref, ref, sem).wait()

    def sent(q):
        if q == 0:
            wait_blocks(CHIPS - 1, send_sem.at[0])
            return

        @pl.when(core == goals[q])
        def _():
            wait_blocks(CHIPS - 1, send_sem.at[q])

        @pl.when(core != goals[q])
        def _():
            wait_blocks(CHIPS, send_sem.at[q])

    def passing():
        half = x.at[0, :, core]
        return remote(half, half, pass_send, pass_recv, sibling)

    def place(owner, piece, i):
        diagonal = owner + 2 * lax.rem(piece // 2 + channel // 8, 2)
        return i * 8 + lax.rem(piece + channel // 4, 2) * 4 + lax.rem(diagonal + 4 - i, 4)

    def far_start(piece):
        for i in range(4):
            block = part.at[place(1 - group, piece, i)]
            remote(block, far.at[piece, i], far_send.at[piece], far_recv.at[piece], partner).start()

    def far_wait(piece, sem):
        ref = far.at[piece]
        pltpu.make_async_copy(ref, ref, sem.at[piece]).wait()

    def far_next(piece):
        far_wait(piece - 1, far_send)
        far_start(piece)

    def settle(piece):
        far_wait(piece, far_recv)

        def one(i, carry):
            other = place(group, piece, i)
            part[other] = part[other] + far[piece, i]
            for half in range(2):
                block, goal = part.at[other, half], landed.at[1, channel]
                if half == 0:
                    remote(block, goal, out_send.at[1], out_recv.at[1], {"seq": other * 2 + half}).start()
                else:

                    @pl.when(other != chip)
                    def _():
                        remote(block, goal, out_send.at[1], out_recv.at[1], {"seq": other * 2 + half}).start()

                    @pl.when(other == chip)
                    def _():
                        pltpu.make_async_copy(block, goal, out_own).start()

                device = {"dp": 1 - group, "seq": other * 2 + half}
                remote(block, goal, out_send.at[1], out_recv.at[1], device).start()
            return carry

        lax.fori_loop(0, 4, one, 0)

    def gradient(step, carry):
        other = jnp.bitwise_xor(chip, step)
        for half in range(2):
            device = {"seq": other * 2 + half}
            remote(part.at[other, half], landed.at[0, channel], out_send.at[0], out_recv.at[0], device).start()
        return carry

    own_out = pltpu.make_async_copy(part.at[chip, core], landed.at[core, channel], out_own)

    roll(0)
    pl.semaphore_wait(barrier, CHIPS + 1)
    scatter(0)
    pl.semaphore_signal(ready, inc=1, device_id=sibling, device_id_type=MESH)
    roll(1)
    roll(2)
    pl.semaphore_wait(ready, 1)
    sent(0)
    scatter(1)
    own(0).wait()
    wait_blocks(CHIPS - 1, recv_sem.at[0])
    passing().start()
    for load in loads:
        load.wait()
    passing().wait_recv()
    forward(x.at[0], rows, twiddle, lanes, work, spec.at[0])
    sent(1)
    scatter(2)

    @pl.when(core == 0)
    def _():
        own(2).wait()

    @pl.when(core == 1)
    def _():
        own(1).wait()

    wait_blocks(2 * CHIPS - 1, recv_sem.at[1])
    forward(x.at[1], rows, twiddle, lanes, work, spec.at[1])
    backward(spec.at[0], spec.at[1], rows_back, twiddle, lanes_back, wide, part)

    @pl.when(core == 0)
    def _():
        own_out.start()
        remote(part.at[chip, 1], landed.at[0, channel], out_send.at[0], out_recv.at[0], sibling).start()
        lax.fori_loop(1, CHIPS, gradient, 0)

    @pl.when(core == 1)
    def _():
        far_start(0)
        for piece in range(4):
            if piece < 3:
                far_next(piece + 1)
            settle(piece)
        far_wait(3, far_send)

    passing().wait_send()
    sent(2)

    @pl.when(core == 0)
    def _():
        own_out.wait()
        wait_blocks(2 * CHIPS - 1, out_send.at[0])
        wait_blocks(CHIPS - 1, out_recv.at[0])

    @pl.when(core == 1)
    def _():
        wait_blocks(CHIPS, out_recv.at[0])

        @pl.when(side == group)
        def _():
            own_out.wait()
            wait_blocks(2 * CHIPS - 1, out_send.at[1])

        @pl.when(side != group)
        def _():
            wait_blocks(2 * CHIPS, out_send.at[1])

    @pl.when(jnp.logical_and(core == 1, side == group))
    def _():
        wait_blocks(CHIPS - 1, out_recv.at[1])

    @pl.when(jnp.logical_or(core == 0, side != group))
    def _():
        wait_blocks(CHIPS, out_recv.at[1])


def finish(landed, grad, skip, grad_in, filter_grad):
    channels = grad.shape[0]
    shape = (channels, skip.shape[1])
    chosen = lax.broadcasted_iota(jnp.int32, shape, 1) == (
        lax.broadcasted_iota(jnp.int32, shape, 0) + pl.program_id(0) * channels
    )
    gain = jnp.sum(jnp.where(chosen, skip[...], 0.0), axis=1, keepdims=True)
    for n in range(ROWS):
        at = slice(n * COLS, (n + 1) * COLS)
        grad_in[:, at] = landed[0, :, n, :] + gain * grad[:, at]
        filter_grad[:, at] = landed[1, :, n, :]


def shards(inputs, grad_out, filters, skip):
    channels, length = filters.shape
    constants = tables()
    vmem, dma = pltpu.VMEM, pltpu.SemaphoreType.DMA
    any_space = pl.BlockSpec(memory_space=pl.ANY)
    grad = grad_out.reshape(channels, length)
    landed = pl.pallas_call(
        kernel,
        out_shape=jax.ShapeDtypeStruct((2, CHIPS, ROWS, COLS), jnp.float32),
        in_specs=[any_space] * 8,
        out_specs=any_space,
        scratch_shapes=[
            vmem((3, channels, length), jnp.float32),
            vmem((3, CHIPS, ROWS, COLS), jnp.float32),
            vmem((2, CHIPS, 2, ROWS, COLS), jnp.float32),
            vmem((2, 2, 4, 4 * RAD, 2 * RAD), jnp.float32),
            vmem((2, 2, 4 * RAD, COLS), jnp.float32),
            vmem((2, 4, 2, 2 * RAD, COLS), jnp.bfloat16),
            vmem((CHIPS, 2, ROWS, COLS), jnp.float32),
            vmem((4, 4, 2, ROWS, COLS), jnp.float32),
            vmem(constants[0].shape, jnp.bfloat16),
            vmem(constants[1].shape, jnp.bfloat16),
            vmem(constants[2].shape, jnp.float32),
            vmem(constants[3].shape, jnp.bfloat16),
            vmem(constants[4].shape, jnp.bfloat16),
            dma((5,)), dma((3,)), dma((3,)), dma((3,)), dma((2,)), dma(()), dma(()), pltpu.SemaphoreType.REGULAR,
            dma((4,)), dma((4,)), dma((2,)), dma((2,)), dma(()),
        ],
        compiler_params=pltpu.CompilerParams(
            collective_id=0, has_side_effects=True, vmem_limit_bytes=56 * 2**20
        ),
        cost_estimate=pl.CostEstimate(flops=11 * 10**9, bytes_accessed=2 * 10**7, transcendentals=0),
    )(
        grad, inputs.reshape(channels, length), filters,
        *(jnp.asarray(table) for table in constants),
    )
    flat = pl.BlockSpec((16, length), lambda i: (i, 0))
    grad_in, filter_grad = pl.pallas_call(
        finish,
        out_shape=[jax.ShapeDtypeStruct((channels, length), jnp.float32)] * 2,
        grid=(channels // 16,),
        in_specs=[
            pl.BlockSpec((2, 16, ROWS, COLS), lambda i: (0, i, 0, 0)),
            flat,
            pl.BlockSpec((1, channels), lambda i: (0, 0)),
        ],
        out_specs=[flat, flat],
        cost_estimate=pl.CostEstimate(flops=10**6, bytes_accessed=5 * 2**20, transcendentals=0),
    )(landed, grad, skip.reshape(1, channels))
    return (grad_in.reshape(1, channels, length), filter_grad)


def solution(mesh):
    return jax.shard_map(
        shards,
        mesh=mesh,
        in_specs=(P("dp", None, "seq"), P("dp", None, "seq"), P(None, "seq"), P()),
        out_specs=(P("dp", None, "seq"), P(None, "seq")),
        check_vma=False,
    )
```

time: 93.8 us -> 88.4 us (0.942)
  the two profiles are of different devices: /device:TPU:24 before, /device:TPU:1 now
where the time goes in v3:
time: 88.4 us; the launch traced here: 88.3 us
  Pallas kernels  87.6 us (99%)
    pallas_call x1, Pallas kernels, shards(): pl.pallas_call(kernel, out_shape=jax.ShapeDtypeStruct((2, CHIPS, ROWS, CO...  84.5 us
    pallas_call x1, Pallas kernels, shards(): pl.pallas_call(finish, out_shape=[jax.ShapeDtypeStruct((channels, length)...  3.09 us

profile of v3, /device:TPU:1, one launch (start us, length us, event | category | flops | bytes accessed | tf_op | source)
XLA Modules:
  0.0 88.3 jit_solution(1401190127472113598)
XLA Ops:
  0.6 84.5 %shard_map.104.landed = f32[2,32,16,512]{3,2,1,0:T(8,128)} custom-call(f32[32,8192]{1,0:T(8,128)} %bitcast.4, f32[32,8192]{1,0:T(8,128)} %bitcast.7, f32[32,8192]{1,0:T(8,128)} %filters.1, bf16[2,4,256,768]{3,2,1,0:T(8,128)(2,1)} %constant.10.clone.rows_all, bf16[2,4,256,768]{3,2,1,0:T(8,128)(2,1)} %constant.11.clone.rows_back_all, ...), custom_call_target="tpu_custom_call" | custom-call | flops 11000000512 | bytes 20000000 | tf_op jit(solution)/shard_map/pallas_call | solution.py:402
  85.2 3.1 %shard_map.105 = (f32[32,8192]{1,0:T(8,128)}, f32[32,8192]{1,0:T(8,128)}) custom-call(f32[2,32,16,512]{3,2,1,0:T(8,128)} %shard_map.104.landed, f32[32,8192]{1,0:T(8,128)} %bitcast.5, f32[1,32]{1,0:T(1,128)} %bitcast.6), custom_call_target="tpu_custom_call" | custom-call | flops 1000000 | bytes 5242880 | tf_op jit(solution)/shard_map/pallas_call | solution.py:433

commit v4 on v3

--- a/solution.py
+++ b/solution.py
@@ -211,7 +211,7 @@
 
     def scatter(q):
         def one(step, carry):
-            other = jnp.bitwise_xor(chip, step)
+            other = jnp.bitwise_xor(chip, lax.rem(step * 11, CHIPS))
             block = rolled.at[q, jnp.bitwise_xor(other, flip)]
             device = {"seq": other * 2 + goals[q]}
             remote(block, slot(q), send_sem.at[q], recv_sem.at[min(q, 1)], device).start()
@@ -271,34 +271,37 @@
     def settle(piece):
         far_wait(piece, far_recv)
 
-        def one(i, carry):
+        def add(i, carry):
             other = place(group, piece, i)
             part[other] = part[other] + far[piece, i]
-            for half in range(2):
-                block, goal = part.at[other, half], landed.at[1, channel]
-                if half == 0:
-                    remote(block, goal, out_send.at[1], out_recv.at[1], {"seq": other * 2 + half}).start()
-                else:
-
-                    @pl.when(other != chip)
-                    def _():
-                        remote(block, goal, out_send.at[1], out_recv.at[1], {"seq": other * 2 + half}).start()
-
-                    @pl.when(other == chip)
-                    def _():
-                        pltpu.make_async_copy(block, goal, out_own).start()
-
-                device = {"dp": 1 - group, "seq": other * 2 + half}
-                remote(block, goal, out_send.at[1], out_recv.at[1], device).start()
             return carry
 
-        lax.fori_loop(0, 4, one, 0)
+        def one(step, carry):
+            other = place(group, piece, lax.rem(step + chip // 8, 4))
+            half = step // 4
+            block, goal = part.at[other, half], landed.at[1, channel]
+            device = {"dp": 1 - group, "seq": other * 2 + half}
+            remote(block, goal, out_send.at[1], out_recv.at[1], device).start()
+            mine = jnp.logical_and(other == chip, half == 1)
+
+            @pl.when(jnp.logical_not(mine))
+            def _():
+                remote(block, goal, out_send.at[1], out_recv.at[1], {"seq": other * 2 + half}).start()
+
+            @pl.when(mine)
+            def _():
+                pltpu.make_async_copy(block, goal, out_own).start()
+
+            return carry
+
+        lax.fori_loop(0, 4, add, 0)
+        lax.fori_loop(0, 8, one, 0)
 
     def gradient(step, carry):
-        other = jnp.bitwise_xor(chip, step)
-        for half in range(2):
-            device = {"seq": other * 2 + half}
-            remote(part.at[other, half], landed.at[0, channel], out_send.at[0], out_recv.at[0], device).start()
+        other = jnp.bitwise_xor(chip, lax.rem((1 + lax.rem(step, CHIPS - 1)) * 11, CHIPS))
+        half = step // (CHIPS - 1)
+        block = part.at[other, half]
+        remote(block, landed.at[0, channel], out_send.at[0], out_recv.at[0], {"seq": other * 2 + half}).start()
         return carry
 
     own_out = pltpu.make_async_copy(part.at[chip, core], landed.at[core, channel], out_own)
@@ -338,7 +341,7 @@
     def _():
         own_out.start()
         remote(part.at[chip, 1], landed.at[0, channel], out_send.at[0], out_recv.at[0], sibling).start()
-        lax.fori_loop(1, CHIPS, gradient, 0)
+        lax.fori_loop(0, 2 * CHIPS - 2, gradient, 0)
 
     @pl.when(core == 1)
     def _():

time: 88.4 us -> 84.3 us (0.954)
  Pallas kernels: 87.6 us -> 83.6 us
    pallas_call x1, Pallas kernels: 84.5 us -> 80.5 us  [shards(): pl.pallas_call(kernel, out_shape=jax.ShapeDtypeStruct((2, CHIPS, ROWS, CO...]
where the time goes in v4:
time: 84.3 us; the launch traced here: 84.2 us
  Pallas kernels  83.6 us (99%)
    pallas_call x1, Pallas kernels, shards(): pl.pallas_call(kernel, out_shape=jax.ShapeDtypeStruct((2, CHIPS, ROWS, CO...  80.5 us
    pallas_call x1, Pallas kernels, shards(): pl.pallas_call(finish, out_shape=[jax.ShapeDtypeStruct((channels, length)...  3.09 us

profile of v4, /device:TPU:1, one launch (start us, length us, event | category | flops | bytes accessed | tf_op | source)
XLA Modules:
  0.0 84.2 jit_solution(488014020419304098)
XLA Ops:
  0.6 80.5 %shard_map.104.landed = f32[2,32,16,512]{3,2,1,0:T(8,128)} custom-call(f32[32,8192]{1,0:T(8,128)} %bitcast.4, f32[32,8192]{1,0:T(8,128)} %bitcast.7, f32[32,8192]{1,0:T(8,128)} %filters.1, bf16[2,4,256,768]{3,2,1,0:T(8,128)(2,1)} %constant.10.clone.rows_all, bf16[2,4,256,768]{3,2,1,0:T(8,128)(2,1)} %constant.11.clone.rows_back_all, ...), custom_call_target="tpu_custom_call" | custom-call | flops 11000000512 | bytes 20000000 | tf_op jit(solution)/shard_map/pallas_call | solution.py:405
  81.1 3.1 %shard_map.105 = (f32[32,8192]{1,0:T(8,128)}, f32[32,8192]{1,0:T(8,128)}) custom-call(f32[2,32,16,512]{3,2,1,0:T(8,128)} %shard_map.104.landed, f32[32,8192]{1,0:T(8,128)} %bitcast.5, f32[1,32]{1,0:T(1,128)} %bitcast.6), custom_call_target="tpu_custom_call" | custom-call | flops 1000000 | bytes 5242880 | tf_op jit(solution)/shard_map/pallas_call | solution.py:436

commit v5 on v4

--- a/solution.py
+++ b/solution.py
@@ -175,8 +175,7 @@
         )
 
     raws = [pltpu.make_async_copy(signals[q], raw.at[q], raw_sem.at[q]) for q in range(3)]
-    for copy in raws:
-        copy.start()
+    raws[0].start()
     loads = [
         pltpu.make_async_copy(rows_all, rows, table_sem.at[0]),
         pltpu.make_async_copy(twiddle_all, twiddle, table_sem.at[1]),
@@ -184,19 +183,18 @@
         pltpu.make_async_copy(lanes_back_all, lanes_back, table_sem.at[3]),
         pltpu.make_async_copy(rows_back_all, rows_back, table_sem.at[4]),
     ]
-    for load in loads:
-        load.start()
-
     barrier = pltpu.get_barrier_semaphore()
 
     def greet(step, carry):
-        other = jnp.bitwise_xor(chip, step) * 2 + core
+        other = jnp.bitwise_xor(chip, CHIPS - step) * 2 + core
         pl.semaphore_signal(barrier, inc=1, device_id={"seq": other}, device_id_type=MESH)
         return carry
 
     lax.fori_loop(1, CHIPS, greet, 0)
     for other in (sibling, partner):
         pl.semaphore_signal(barrier, inc=1, device_id=other, device_id_type=MESH)
+    for copy in raws[1:] + loads:
+        copy.start()
 
     def roll(q):
         raws[q].wait()
@@ -278,7 +276,7 @@
 
         def one(step, carry):
             other = place(group, piece, lax.rem(step + chip // 8, 4))
-            half = step // 4
+            half = lax.rem(step // 4 + step, 2)
             block, goal = part.at[other, half], landed.at[1, channel]
             device = {"dp": 1 - group, "seq": other * 2 + half}
             remote(block, goal, out_send.at[1], out_recv.at[1], device).start()
@@ -299,7 +297,7 @@
 
     def gradient(step, carry):
         other = jnp.bitwise_xor(chip, lax.rem((1 + lax.rem(step, CHIPS - 1)) * 11, CHIPS))
-        half = step // (CHIPS - 1)
+        half = lax.rem(step // (CHIPS - 1) + lax.rem(step, CHIPS - 1), 2)
         block = part.at[other, half]
         remote(block, landed.at[0, channel], out_send.at[0], out_recv.at[0], {"seq": other * 2 + half}).start()
         return carry

time: 84.3 us -> 83.6 us (level)
  no operation moved by 1% of the time
where the time goes in v5:
time: 83.6 us; the launch traced here: 83.5 us
  Pallas kernels  82.9 us (99%)
    pallas_call x1, Pallas kernels, shards(): pl.pallas_call(kernel, out_shape=jax.ShapeDtypeStruct((2, CHIPS, ROWS, CO...  79.8 us
    pallas_call x1, Pallas kernels, shards(): pl.pallas_call(finish, out_shape=[jax.ShapeDtypeStruct((channels, length)...  3.09 us

profile of v5, /device:TPU:1, one launch (start us, length us, event | category | flops | bytes accessed | tf_op | source)
XLA Modules:
  0.0 83.5 jit_solution(17420130712364748865)
XLA Ops:
  0.6 79.8 %shard_map.104.landed = f32[2,32,16,512]{3,2,1,0:T(8,128)} custom-call(f32[32,8192]{1,0:T(8,128)} %bitcast.4, f32[32,8192]{1,0:T(8,128)} %bitcast.7, f32[32,8192]{1,0:T(8,128)} %filters.1, bf16[2,4,256,768]{3,2,1,0:T(8,128)(2,1)} %constant.10.clone.rows_all, bf16[2,4,256,768]{3,2,1,0:T(8,128)(2,1)} %constant.11.clone.rows_back_all, ...), custom_call_target="tpu_custom_call" | custom-call | flops 11000000512 | bytes 20000000 | tf_op jit(solution)/shard_map/pallas_call | solution.py:403
  80.4 3.1 %shard_map.105 = (f32[32,8192]{1,0:T(8,128)}, f32[32,8192]{1,0:T(8,128)}) custom-call(f32[2,32,16,512]{3,2,1,0:T(8,128)} %shard_map.104.landed, f32[32,8192]{1,0:T(8,128)} %bitcast.5, f32[1,32]{1,0:T(1,128)} %bitcast.6), custom_call_target="tpu_custom_call" | custom-call | flops 1000000 | bytes 5242880 | tf_op jit(solution)/shard_map/pallas_call | solution.py:434

commit v6 on v5

--- a/solution.py
+++ b/solution.py
@@ -215,7 +215,7 @@
             remote(block, slot(q), send_sem.at[q], recv_sem.at[min(q, 1)], device).start()
             return carry
 
-        lax.fori_loop(1, CHIPS, one, 0)
+        lax.fori_loop(1, CHIPS, one, 0, unroll=True)
         if q == 0:
             own(q).start()
             return

time: 83.6 us -> 83.5 us (level)
  no operation moved by 1% of the time
where the time goes in v6:
time: 83.5 us; the launch traced here: 83.4 us
  Pallas kernels  82.8 us (99%)
    pallas_call x1, Pallas kernels, shards(): pl.pallas_call(kernel, out_shape=jax.ShapeDtypeStruct((2, CHIPS, ROWS, CO...  79.7 us
    pallas_call x1, Pallas kernels, shards(): pl.pallas_call(finish, out_shape=[jax.ShapeDtypeStruct((channels, length)...  3.09 us

profile of v6, /device:TPU:1, one launch (start us, length us, event | category | flops | bytes accessed | tf_op | source)
XLA Modules:
  0.0 83.4 jit_solution(13833133990426689559)
XLA Ops:
  0.6 79.7 %shard_map.104.landed = f32[2,32,16,512]{3,2,1,0:T(8,128)} custom-call(f32[32,8192]{1,0:T(8,128)} %bitcast.4, f32[32,8192]{1,0:T(8,128)} %bitcast.7, f32[32,8192]{1,0:T(8,128)} %filters.1, bf16[2,4,256,768]{3,2,1,0:T(8,128)(2,1)} %constant.10.clone.rows_all, bf16[2,4,256,768]{3,2,1,0:T(8,128)(2,1)} %constant.11.clone.rows_back_all, ...), custom_call_target="tpu_custom_call" | custom-call | flops 11000000512 | bytes 20000000 | tf_op jit(solution)/shard_map/pallas_call | solution.py:403
  80.3 3.1 %shard_map.105 = (f32[32,8192]{1,0:T(8,128)}, f32[32,8192]{1,0:T(8,128)}) custom-call(f32[2,32,16,512]{3,2,1,0:T(8,128)} %shard_map.104.landed, f32[32,8192]{1,0:T(8,128)} %bitcast.5, f32[1,32]{1,0:T(1,128)} %bitcast.6), custom_call_target="tpu_custom_call" | custom-call | flops 1000000 | bytes 5242880 | tf_op jit(solution)/shard_map/pallas_call | solution.py:434
